TPU v7x, 32 devices: a whole 2x2x4 slice. The times are simulated.
32 devices in a mesh: section: 4 (over z), row: 4 (over y, x), col: 2 (over core).
Axes of the slice: x: 2, y: 2, z: 4, core: 2. Of those that a mesh axis runs over, the one named last changes fastest.
Arguments:
- act_in: bfloat16 [4, 8, 12288], P('section', 'row', 'col'), may hold values from -6 to 6
- hid_in: bfloat16 [4, 8, 1536], P('section', None, 'row'), may hold values from -6 to 6
- grad_in: bfloat16 [4, 8, 12288], P('section', 'row', 'col'), may hold values from -6 to 6
- saved_in: bfloat16 [4, 8, 12288], P('section', 'row', 'col'), may hold values from -6 to 6
- saved_pre: bfloat16 [4, 8, 1536], P('section', None, 'row'), may hold values from -6 to 6
- weights: bfloat16 [4, 12288, 1536], P('section', 'col', 'row'), may hold values from -0.0546875 to 0.0546875
- norm_gain: float32 [2, 12288], P(None, 'col'), may hold values from 0.25 to 1.75
- norm_bias: float32 [2, 12288], P(None, 'col'), may hold values from -0.5 to 0.5
Outputs:
- act_out: bfloat16 [4, 8, 12288], P('section', 'row', 'col')
- hid_out: bfloat16 [4, 8, 1536], P('section', None, 'row')
- grad_out: bfloat16 [4, 8, 12288], P('section', 'row', 'col')
All inputs are finite; a program needn't handle non-finite values.
Results may differ from a plain program's by a relative error of at most 0.0035.
Values may be sent and summed in bfloat16 or wider, within the bound.
A program may use at most 64 MiB of HBM per device.

v0:
```python
import jax
import jax.numpy as jnp
from jax import lax
from jax.sharding import PartitionSpec as P

D = 12288


epsilon = 1e-05


def passed_along(block, axis, distance):
    devices = range(lax.axis_size(axis))
    route = [((i - distance) % len(devices), i) for i in devices]
    return lax.ppermute(block, axis, route)


def partner(shard, axis, stride):
    return lax.ppermute(shard, axis, [(i, i ^ 1 << stride) for i in range(lax.axis_size(axis))])


def col_total(values):
    return lax.psum(values, "col")


def boundary(values, offset):
    return passed_along(values, "section", offset)


def statistics(total, squares):
    average = total / D
    inverse_scale = lax.rsqrt(squares / D - average * average + epsilon)
    return (average[:, None], inverse_scale[:, None])


def gelu_slope(preact, upstream):
    return jax.vjp(lambda value: jax.nn.gelu(value, approximate=True), preact)[1](upstream)[0]


def per_device(act_in, hid_in, grad_in, saved_in, saved_pre, weights, norm_gain, norm_bias):
    section_index = lax.axis_index("section")
    is_even = section_index % 2 == 0
    layer = section_index // 2
    gain = lax.dynamic_index_in_dim(norm_gain, layer, 0, keepdims=False)
    offset_bias = lax.dynamic_index_in_dim(norm_bias, layer, 0, keepdims=False)
    weight = weights[0]
    stream = act_in[0]
    gradient = grad_in[0]
    stream_float = stream.astype(jnp.float32)
    saved_float = saved_in[0].astype(jnp.float32)
    sums = col_total(
        (
            jnp.sum(stream_float, axis=-1),
            jnp.sum(stream_float * stream_float, axis=-1),
            jnp.sum(saved_float, axis=-1),
            jnp.sum(saved_float * saved_float, axis=-1),
        )
    )
    stream_mean, stream_scale = statistics(sums[0], sums[1])
    saved_mean, saved_scale = statistics(sums[2], sums[3])
    normed = ((stream_float - stream_mean) * stream_scale * gain + offset_bias).astype(jnp.bfloat16)
    leading = jnp.where(is_even, normed, gradient)
    partial_sums = jnp.dot(
        lax.all_gather(leading, "row", axis=0, tiled=True),
        weight,
        preferred_element_type=jnp.float32,
    )
    summed = col_total(partial_sums)
    hidden_value = jnp.where(is_even, jax.nn.gelu(summed, approximate=True), summed).astype(
        jnp.bfloat16
    )
    hidden_next = partner(hidden_value, "section", 0)
    slope = gelu_slope(saved_pre[0].astype(jnp.float32), hid_in[0].astype(jnp.float32)).astype(
        jnp.bfloat16
    )
    right_side = jnp.where(is_even, slope, hid_in[0])
    term = lax.psum_scatter(
        lax.dot_general(
            right_side, weight, (((1,), (1,)), ((), ())), preferred_element_type=jnp.float32
        ),
        "row",
        scatter_dimension=0,
        tiled=True,
    )
    forward_odd = (stream_float + term).astype(jnp.bfloat16)
    saved_hat = (saved_float - saved_mean) * saved_scale
    scaled = term * gain
    moments = col_total((jnp.sum(scaled, axis=-1), jnp.sum(scaled * saved_hat, axis=-1)))
    first_mean = (moments[0] / D)[:, None]
    second_mean = (moments[1] / D)[:, None]
    backward_even = (
        gradient.astype(jnp.float32) + saved_scale * (scaled - first_mean - saved_hat * second_mean)
    ).astype(jnp.bfloat16)
    forward_value = jnp.where(is_even, stream, forward_odd)
    backward_value = jnp.where(is_even, backward_even, gradient)
    act_next = boundary(forward_value, 1)
    grad_next = boundary(backward_value, -1)
    return (act_next[None], hidden_next[None], grad_next[None])


def solution(mesh):
    in_specs = (
        P("section", "row", "col"),
        P("section", None, "row"),
        P("section", "row", "col"),
        P("section", "row", "col"),
        P("section", None, "row"),
        P("section", "col", "row"),
        P(None, "col"),
        P(None, "col"),
    )
    out_specs = (P("section", "row", "col"), P("section", None, "row"), P("section", "row", "col"))
    return jax.shard_map(
        per_device, mesh=mesh, in_specs=in_specs, out_specs=out_specs, check_vma=False
    )
```

profile of v0, /device:TPU:0, one launch (start us, length us, event | category | flops | bytes accessed | tf_op | source)
XLA Modules:
  0.0 79.1 jit_solution(15966183395341835067)
XLA Ops:
  7.2 0.0 copy-start
  7.2 0.0 copy-start.4
  7.2 0.0 copy-start.1
  7.2 0.0 copy-start.2
  7.2 0.0 copy-start.3
  7.2 0.0 all-reduce.5.cloned.1.call-start
  7.3 0.0 copy-start.5
  7.3 4.4 %fusion.2 = f32[8,6144]{1,0:T(8,128)} fusion(bf16[1,6144,384]{2,1,0:T(8,128)(2,1)} %param.13, bf16[1,8,384]{2,1,0:T(8,128)(2,1)} %param.9, bf16[1,8,384]{2,1,0:T(8,128)(2,1)} %param.12, pred[]{:T(512)S(6)} %eq.5), kind=kOutput, calls=%fused_computation.2 | convolution fusion | flops 37819392 | bytes 4927489 | tf_op jit(solution)/shard_map/dot_general | solution.py:78
  11.7 0.0 all-reduce.5.cloned.1.call-update
  11.7 0.0 copy-done
  11.8 0.0 copy-done.4
  11.8 0.2 convert_reduce_fusion.1
  12.0 0.0 copy-done.2
  12.0 0.2 convert_reduce_fusion
  12.2 2.6 %all-reduce.2 = (f32[2]{0:T(128)S(1)}, f32[2]{0:T(128)S(1)}, f32[2]{0:T(128)S(1)}, f32[2]{0:T(128)S(1)}) all-reduce(f32[2]{0:T(128)S(1)} %get-tuple-element.6, f32[2]{0:T(128)S(1)} %get-tuple-element.5, f32[2]{0:T(128)S(1)} %get-tuple-element.20, f32[2]{0:T(128)S(1)} %convert_reduce_fusion.1), channel_id=1, replica_groups=mesh['section'=4,'row'=4,'col'=2] {'col'}, use_global_device_ids=true, to_apply=%region_4.5 | all-reduce | flops 8 | bytes 64 | tf_op jit(solution)/shard_map/psum | solution.py:23
  14.8 0.1 fusion.14
  14.9 9.7 %all-gather = bf16[4,2,6144]{2,1,0:T(2,128)(2,1)S(1)} all-gather(bf16[1,2,6144]{2,1,0:T(2,128)(2,1)S(1)} %fusion.14), channel_id=1, replica_groups=mesh['section'=4,'row'=4,'col'=2] {'row'}, dimensions={0}, use_global_device_ids=true | all-gather | bytes 122880 | tf_op jit(solution)/shard_map/all_gather | solution.py:64
  24.7 3.0 %fusion = f32[8,384]{1,0:T(8,128)S(1)} fusion(bf16[8,6144]{1,0:T(8,128)(2,1)S(1)} %reshape.15, bf16[1,6144,384]{2,1,0:T(8,128)(2,1)} %param.13), kind=kOutput, calls=%fused_computation | convolution fusion | flops 37748736 | bytes 4829184 | tf_op jit(solution)/shard_map/dot_general | solution.py:63
  27.7 0.6 dynamic-slice
  29.0 28.3 %all-reduce.5.cloned.1.call-done = f32[8,6144]{1,0:T(8,128)} async-done(((f32[8,6144]{1,0:T(8,128)}), f32[8,6144]{1,0:T(8,128)}) %all-reduce.5.cloned.1.call-update) | async-done | bytes 196624
  57.3 1.2 %fusion.47 = (f32[2]{0:T(128)S(1)}, f32[2]{0:T(128)S(1)}) fusion(f32[6144]{0:T(1024)S(1)} %bitcast.46, f32[8,6144]{1,0:T(8,128)} %all-reduce.5.cloned.1.call-done, u32[]{:T(128)S(6)} %multiply.9, f32[2]{0:T(128)S(1)} %get-tuple-element.17, f32[2]{0:T(128)S(1)} %get-tuple-element.16, bf16[1,2,6144]{2,1,0:T(2,128)(2,1)S(1)} %copy-done.1), kind=kLoop, calls=%fused_computation.73 | loop fusion | flops 86012 | bytes 98340 | tf_op jit(solution)/shard_map/reduce_sum | solution.py:88
  58.5 3.3 %all-reduce.1 = (f32[8,384]{1,0:T(8,128)S(1)}, f32[2]{0:T(128)S(1)}, f32[2]{0:T(128)S(1)}) all-reduce(f32[8,384]{1,0:T(8,128)S(1)} %fusion, f32[2]{0:T(128)S(1)} %get-tuple-element.4, f32[2]{0:T(128)S(1)} %get-tuple-element.3), channel_id=1, replica_groups=mesh['section'=4,'row'=4,'col'=2] {'col'}, use_global_device_ids=true, to_apply=%region_5.6 | all-reduce | flops 3076 | bytes 24608 | tf_op jit(solution)/shard_map/psum | solution.py:23
  61.8 1.1 %broadcast_select_fusion = (bf16[2,6144]{1,0:T(2,128)(2,1)S(1)}, bf16[2,6144]{1,0:T(2,128)(2,1)S(1)}) fusion(pred[]{:T(512)S(6)} %eq.5, bf16[1,2,6144]{2,1,0:T(2,128)(2,1)S(1)} %copy-done.1, f32[2]{0:T(128)S(1)} %broadcast_multiply_fusion, f32[2]{0:T(128)S(1)} %get-tuple-element.16, f32[2]{0:T(128)S(1)} %broadcast_multiply_fusion.1, ...), kind=kLoop, calls=%fused_computation.22 | loop fusion | flops 196608 | bytes 196645 | tf_op jit(solution)/shard_map/jit(_where)/select_n | solution.py:95
  62.9 1.5 %collective-permute-start = (bf16[2,6144]{1,0:T(2,128)(2,1)S(1)}, bf16[2,6144]{1,0:T(2,128)(2,1)S(1)}, u32[]{:S(2)}, u32[]{:S(2)}) collective-permute-start(bf16[2,6144]{1,0:T(2,128)(2,1)S(1)} %get-tuple-element.15), channel_id=1, source_target_pairs={{24,0},{0,8},{8,16},{16,24},{25,1},{1,9},{9,17},{17,25},{26,2},{2,... | collective-permute-start | bytes 73736 | tf_op jit(solution)/shard_map/ppermute | solution.py:15
  64.4 2.3 %collective-permute-start.2 = (bf16[2,6144]{1,0:T(2,128)(2,1)S(1)}, bf16[2,6144]{1,0:T(2,128)(2,1)S(1)}, u32[]{:S(2)}, u32[]{:S(2)}) collective-permute-start(bf16[2,6144]{1,0:T(2,128)(2,1)S(1)} %get-tuple-element.14), channel_id=1, source_target_pairs={{8,0},{16,8},{24,16},{0,24},{9,1},{17,9},{25,17},{1,25},{10,2},{18... | collective-permute-start | bytes 73736 | tf_op jit(solution)/shard_map/ppermute | solution.py:15
  66.8 0.1 collective-permute-start.1
  66.8 3.6 %collective-permute-done.1 = bf16[8,384]{1,0:T(8,128)(2,1)S(1)} collective-permute-done((bf16[8,384]{1,0:T(8,128)(2,1)S(1)}, bf16[8,384]{1,0:T(8,128)(2,1)S(1)}, u32[]{:S(2)}, u32[]{:S(2)}) %collective-permute-start.1) | collective-permute-done | bytes 6176 | tf_op jit(solution)/shard_map/ppermute | solution.py:19
  70.5 0.0 collective-permute-done
  70.5 0.0 collective-permute-done.2
  70.5 0.6 copy.15
  71.1 0.6 copy.16
  71.7 0.6 copy.17
  (11 shorter events, 0.1 us)
Async XLA Ops:
  7.2 4.6 %copy-start = (f32[2,6144]{1,0:T(2,128)S(1)}, f32[2,6144]{1,0:T(2,128)}, u32[]{:S(2)}) copy-start(f32[2,6144]{1,0:T(2,128)} %param.14) | copy-start | bytes 147460
  7.2 4.6 %copy-start.4 = (f32[2,6144]{1,0:T(2,128)S(1)}, f32[2,6144]{1,0:T(2,128)}, u32[]{:S(2)}) copy-start(f32[2,6144]{1,0:T(2,128)} %param.15) | copy-start | bytes 147460
  7.2 4.6 %copy-start.1 = (bf16[1,2,6144]{2,1,0:T(2,128)(2,1)S(1)}, bf16[1,2,6144]{2,1,0:T(2,128)(2,1)}, u32[]{:S(2)}) copy-start(bf16[1,2,6144]{2,1,0:T(2,128)(2,1)} %param.11) | copy-start | bytes 73732
  7.2 4.8 %copy-start.2 = (bf16[1,2,6144]{2,1,0:T(2,128)(2,1)S(1)}, bf16[1,2,6144]{2,1,0:T(2,128)(2,1)}, u32[]{:S(2)}) copy-start(bf16[1,2,6144]{2,1,0:T(2,128)(2,1)} %param.8) | copy-start | bytes 73732
  7.2 7.6 %copy-start.3 = (bf16[1,2,6144]{2,1,0:T(2,128)(2,1)S(1)}, bf16[1,2,6144]{2,1,0:T(2,128)(2,1)}, u32[]{:S(2)}) copy-start(bf16[1,2,6144]{2,1,0:T(2,128)(2,1)} %param.10) | copy-start | bytes 73732
  7.2 50.1 %all-reduce.5.cloned.1.call-start = ((), (), s32[]{:S(2)}) async-start(), calls=%async_computation | async-start | bytes 393216
  7.3 20.5 %copy-start.5 = (u32[32]{0:T(128)S(1)}, u32[32]{0:T(128)}, u32[]{:S(2)}) copy-start(u32[32]{0:T(128)} %constant.68) | copy-start | bytes 388
  62.9 7.6 %collective-permute-start = (bf16[2,6144]{1,0:T(2,128)(2,1)S(1)}, bf16[2,6144]{1,0:T(2,128)(2,1)S(1)}, u32[]{:S(2)}, u32[]{:S(2)}) collective-permute-start(bf16[2,6144]{1,0:T(2,128)(2,1)S(1)} %get-tuple-element.15), channel_id=1, source_target_pairs={{24,0},{0,8},{8,16},{16,24},{25,1},{1,9},{9,17},{17,25},{26,2},{2,... | collective-permute-start | bytes 73736 | tf_op jit(solution)/shard_map/ppermute | solution.py:15
  64.4 6.1 %collective-permute-start.2 = (bf16[2,6144]{1,0:T(2,128)(2,1)S(1)}, bf16[2,6144]{1,0:T(2,128)(2,1)S(1)}, u32[]{:S(2)}, u32[]{:S(2)}) collective-permute-start(bf16[2,6144]{1,0:T(2,128)(2,1)S(1)} %get-tuple-element.14), channel_id=1, source_target_pairs={{8,0},{16,8},{24,16},{0,24},{9,1},{17,9},{25,17},{1,25},{10,2},{18... | collective-permute-start | bytes 73736 | tf_op jit(solution)/shard_map/ppermute | solution.py:15
  66.8 3.7 %collective-permute-start.1 = (bf16[8,384]{1,0:T(8,128)(2,1)S(1)}, bf16[8,384]{1,0:T(8,128)(2,1)S(1)}, u32[]{:S(2)}, u32[]{:S(2)}) collective-permute-start(bf16[8,384]{1,0:T(8,128)(2,1)S(1)} %fusion.26), channel_id=1, source_target_pairs={{0,8},{8,0},{16,24},{24,16},{1,9},{9,1},{17,25},{25,17},{2,10},{10... | collective-permute-start | bytes 18440 | tf_op jit(solution)/shard_map/ppermute | solution.py:19
Sparse Core Ops, SparseCore 0:
  11.8 45.4 all-reduce.4
where the time goes:
time: 79.4 us; the launch traced here: 79.1 us
  waiting for transfers between devices  31.9 us (40%)
  blocking collectives  15.6 us (20%)
  between operations  14.9 us (19%)
  matrix products  7.45 us (9%)
  starting transfers between devices  3.99 us (5%)
  other arithmetic  2.8 us (4%)
  local copies, waits for them, and re-layouts  2.53 us (3%)
    unnamed x2, waiting for transfers between devices  28.3 us
    all_gather x1, blocking collectives, per_device(): lax.all_gather(leading, 'row', axis=0, tiled=True)  9.7 us
    psum x2, blocking collectives, col_total(): return lax.psum(values, 'col')  5.88 us
    dot_general x1, matrix products, per_device(): lax.dot_general(right_side, weight, (((1,), (1,)), ((), ())), preferred_e...  4.4 us
    ppermute x2, starting transfers between devices, passed_along(): return lax.ppermute(block, axis, route)  3.88 us
    ppermute x1, waiting for transfers between devices, partner(): lax.ppermute(shard, axis, [(i, i ^ 1 << stride) for i in range(lax.axis_s...  3.62 us
    dot_general x1, matrix products, per_device(): jnp.dot(lax.all_gather(leading, 'row', axis=0, tiled=True), weight, prefe...  3.05 us
    unnamed x17, local copies, waits for them, and re-layouts  2.48 us
  transfers between devices with their start and end apart: 4, of which 2 were waited for; matrix products, arithmetic and copies ran while one was open for 5% of the time, Pallas kernels for 0%

commit v1 on v0

v1 whole, which is shorter than its diff:
```python
import functools

import jax
import jax.numpy as jnp
from jax import lax
from jax.experimental import pallas as pl
from jax.experimental.pallas import tpu as pltpu
from jax.sharding import PartitionSpec as P

EPSILON = 1e-05
ROOT = 0.7978845608028654
CUBIC = 0.044715
MESH = pl.DeviceIdType.MESH
LANES = 128


def each(count, body):
    if count <= 8:
        for step in range(count):
            body(step)
    else:
        lax.fori_loop(0, count, lambda step, carry: (body(step), carry)[1], 0)


def gelu(x):
    return x * (0.5 * (1.0 + jnp.tanh(ROOT * (x + CUBIC * (x * x * x)))))


def gelu_slope(x):
    t = jnp.tanh(ROOT * (x + CUBIC * (x * x * x)))
    return 0.5 * (1.0 + t) + 0.5 * x * (1.0 - t * t) * (ROOT * (1.0 + 3.0 * CUBIC * (x * x)))


def row_sum(values):
    return jnp.broadcast_to(jnp.sum(values, axis=-1, keepdims=True), (values.shape[0], LANES))


def kernel(
    sizes,
    act_in, hid_in, grad_in, saved_in, pre_in, weights, gain_in, bias_in,
    act_out, hid_out, grad_out,
    w, lead, other, saved, hid, pre, gain, bias, right, x, mean, scale, stats,
    parts, sums, partial, moments, hidden, result,
    w_sem, local_sem, lead_send, lead_recv, stat_send, stat_recv, part_send, part_recv,
    col_send, col_recv, mom_send, mom_recv, edge_send, edge_recv,
):
    S, R, C, own, T, F, DC, N = sizes
    D = DC * C
    K = DC // N
    s, r, c = lax.axis_index("section"), lax.axis_index("row"), lax.axis_index("col")
    even = s % 2 == 0
    odd = s % 2 == 1
    layer = s // 2
    up, down = (s + 1) % S, (s + S - 1) % S
    me = r * C + c

    def local(src, dst, k):
        return pltpu.make_async_copy(src, dst, local_sem.at[k])

    def remote(src, dst, send, recv, **device):
        return pltpu.make_async_remote_copy(
            src_ref=src, dst_ref=dst, send_sem=send, recv_sem=recv,
            device_id=device, device_id_type=MESH,
        )

    @pl.when(even)
    def _():
        local(act_in.at[0], lead.at[r], 0).start()
        local(grad_in.at[0], other, 1).start()

    @pl.when(odd)
    def _():
        local(grad_in.at[0], lead.at[r], 0).start()
        local(act_in.at[0], other, 1).start()

    rest = [(saved_in.at[0], saved, 2), (hid_in.at[0], hid, 3), (pre_in.at[0], pre, 4)]
    rest += [(gain_in, gain, 5), (bias_in, bias, 6)]
    for item in rest:
        local(*item).start()

    def weight_copy(i):
        rows = pl.ds(i * K, K)
        return pltpu.make_async_copy(weights.at[0, rows], w.at[rows], w_sem.at[i])

    for i in range(N):
        weight_copy(i).start()

    barrier = pltpu.get_barrier_semaphore()
    for neighbour in (up, down):
        pl.semaphore_signal(barrier, inc=1, device_id={"section": neighbour}, device_id_type=MESH)

    def place(k):
        to = (me + k + 1) % (R * C)
        return to, {"row": to // C, "col": to % C}

    def greet(k):
        pl.semaphore_signal(barrier, inc=1, device_id=place(k)[1], device_id_type=MESH)

    each(R * C - 1, greet)

    local(act_in.at[0], lead.at[r], 0).wait()
    local(act_in.at[0], other, 1).wait()
    for item in rest:
        local(*item).wait()

    @pl.when(even)
    def _():
        v = lead[r].astype(jnp.float32)
        z = saved[...].astype(jnp.float32)
        stats[me, 0] = row_sum(v)
        stats[me, 1] = row_sum(v * v)
        stats[me, 2] = row_sum(z)
        stats[me, 3] = row_sum(z * z)

    pl.semaphore_wait(barrier, R * C + 1)

    def lead_copy(to):
        return remote(lead.at[r], lead.at[r], lead_send.at[to], lead_recv.at[r], row=to)

    each(R - 1, lambda k: lead_copy((r + k + 1) % R).start())

    def stat_copy(k):
        to, device = place(k)
        return remote(stats.at[me], stats.at[me], stat_send.at[to], stat_recv.at[me], **device)

    @pl.when(even)
    def _():
        each(R * C - 1, lambda k: stat_copy(k).start())

    def act_edge(src, k):
        return remote(src, act_out.at[0], edge_send.at[k], edge_recv.at[0], section=up)

    def grad_edge(src, k):
        return remote(src, grad_out.at[0], edge_send.at[k], edge_recv.at[1], section=down)

    @pl.when(even)
    def _():
        act_edge(lead.at[r], 0).start()
        h = hid[...].astype(jnp.float32)
        right[...] = (h * gelu_slope(pre[...].astype(jnp.float32))).astype(jnp.bfloat16)

    @pl.when(odd)
    def _():
        grad_edge(lead.at[r], 0).start()
        right[...] = hid[...]

    def part_copy(i, to):
        columns = pl.ds(i * K, K)
        return remote(
            parts.at[to, :, columns], sums.at[r, :, columns],
            part_send.at[i, to], part_recv.at[i, r], row=to,
        )

    for i in range(N):
        weight_copy(i).wait()
        term = lax.dot_general(
            right[...], w[i * K:(i + 1) * K, :], (((1,), (1,)), ((), ())),
            preferred_element_type=jnp.float32,
        )
        for q in range(R):
            parts[q, :, i * K:(i + 1) * K] = term[q * own:(q + 1) * own, :]
        each(R - 1, lambda k: part_copy(i, (r + k + 1) % R).start())

    def lead_arrived(k):
        q = (r + k + 1) % R
        remote(lead.at[q], lead.at[q], lead_send.at[q], lead_recv.at[q], row=q).wait_recv()

    each(R - 1, lead_arrived)

    def stat_arrived(k):
        q, device = place(k)
        remote(stats.at[q], stats.at[q], stat_send.at[q], stat_recv.at[q], **device).wait_recv()

    def factors(q, first):
        total, squares = stats[q * C, first], stats[q * C, first + 1]
        for j in range(1, C):
            total = total + stats[q * C + j, first]
            squares = squares + stats[q * C + j, first + 1]
        average = total / D
        return average, lax.rsqrt(squares / D - average * average + EPSILON)

    @pl.when(even)
    def _():
        each(R * C - 1, stat_arrived)
        for q in range(R):
            rows = slice(q * own, (q + 1) * own)
            average, inverse = factors(q, 0)
            mean[rows, :] = average
            scale[rows, :] = inverse

    for q in range(R):
        x[q * own:(q + 1) * own, :] = lead[q].astype(jnp.float32)

    @pl.when(even)
    def _():
        g, b = gain[pl.ds(layer, 1), :], bias[pl.ds(layer, 1), :]
        m, f = mean[:, :1], scale[:, :1]
        for i in range(N):
            columns = slice(i * K, (i + 1) * K)
            x[:, columns] = (x[:, columns] - m) * f * g[:, columns] + b[:, columns]

    total = jnp.zeros((T, F), jnp.float32)
    for i in range(N):
        columns = slice(i * K, (i + 1) * K)
        total = total + jnp.dot(
            x[:, columns].astype(jnp.bfloat16), w[columns, :], preferred_element_type=jnp.float32
        )
    partial[c] = total

    def col_copy(k):
        to = (c + k + 1) % C
        return remote(partial.at[c], partial.at[c], col_send.at[to], col_recv.at[c], col=to)

    each(C - 1, lambda k: col_copy(k).start())

    def part_arrived(k):
        q = (r + k + 1) % R
        for i in range(N):
            columns = pl.ds(i * K, K)
            remote(
                parts.at[q, :, columns], sums.at[q, :, columns],
                part_send.at[i, q], part_recv.at[i, q], row=q,
            ).wait_recv()

    each(R - 1, part_arrived)
    sums[r] = parts[r]
    term = sums[0]
    for q in range(1, R):
        term = term + sums[q]

    @pl.when(odd)
    def _():
        result[...] = (other[...].astype(jnp.float32) + term).astype(jnp.bfloat16)
        act_edge(result, 1).start()

    def mom_copy(k):
        to = (c + k + 1) % C
        return remote(moments.at[c], moments.at[c], mom_send.at[to], mom_recv.at[c], col=to)

    def saved_hat():
        average, inverse = factors(r, 2)
        return (saved[...].astype(jnp.float32) - average[:, :1]) * inverse[:, :1], inverse[:, :1]

    @pl.when(even)
    def _():
        scaled = term * gain[pl.ds(layer, 1), :]
        sums[0] = scaled
        moments[c, 0] = row_sum(scaled)
        moments[c, 1] = row_sum(scaled * saved_hat()[0])
        each(C - 1, lambda k: mom_copy(k).start())

    def col_arrived(k):
        q = (c + k + 1) % C
        remote(partial.at[q], partial.at[q], col_send.at[q], col_recv.at[q], col=q).wait_recv()

    each(C - 1, col_arrived)
    summed = partial[0]
    for q in range(1, C):
        summed = summed + partial[q]

    @pl.when(even)
    def _():
        hidden[...] = gelu(summed).astype(jnp.bfloat16)

    @pl.when(odd)
    def _():
        hidden[...] = summed.astype(jnp.bfloat16)

    pair = s + 1 - 2 * (s % 2)
    hid_copy = remote(hidden, hid_out.at[0], edge_send.at[2], edge_recv.at[2], section=pair)
    hid_copy.start()

    @pl.when(even)
    def _():
        def mom_arrived(k):
            q = (c + k + 1) % C
            remote(moments.at[q], moments.at[q], mom_send.at[q], mom_recv.at[q], col=q).wait_recv()

        each(C - 1, mom_arrived)
        first, second = moments[0, 0], moments[0, 1]
        for q in range(1, C):
            first = first + moments[q, 0]
            second = second + moments[q, 1]
        first, second = first[:, :1] / D, second[:, :1] / D
        h, inverse = saved_hat()
        moved = other[...].astype(jnp.float32) + inverse * (sums[0] - first - h * second)
        result[...] = moved.astype(jnp.bfloat16)
        grad_edge(result, 1).start()

    act_edge(result, 0).wait_recv()
    grad_edge(result, 0).wait_recv()
    hid_copy.wait()
    for k in range(2):
        act_edge(result, k).wait_send()
    each(R - 1, lambda k: lead_copy((r + k + 1) % R).wait_send())
    for i in range(N):
        each(R - 1, lambda k: part_copy(i, (r + k + 1) % R).wait_send())
    each(C - 1, lambda k: col_copy(k).wait_send())

    @pl.when(even)
    def _():
        each(R * C - 1, lambda k: stat_copy(k).wait_send())
        each(C - 1, lambda k: mom_copy(k).wait_send())


def per_device(S, R, C, *arguments):
    act_in, hid_in, grad_in, saved_in, saved_pre, weights, norm_gain, norm_bias = arguments
    own, DC = act_in.shape[1:]
    T, F = hid_in.shape[1:]
    N = 4
    bf16, f32 = jnp.bfloat16, jnp.float32
    dma = pltpu.SemaphoreType.DMA
    scratch = [
        pltpu.VMEM((DC, F), bf16),
        pltpu.VMEM((R, own, DC), bf16),
        pltpu.VMEM((own, DC), bf16),
        pltpu.VMEM((own, DC), bf16),
        pltpu.VMEM((T, F), bf16),
        pltpu.VMEM((T, F), bf16),
        pltpu.VMEM(norm_gain.shape, f32),
        pltpu.VMEM(norm_bias.shape, f32),
        pltpu.VMEM((T, F), bf16),
        pltpu.VMEM((T, DC), f32),
        pltpu.VMEM((T, LANES), f32),
        pltpu.VMEM((T, LANES), f32),
        pltpu.VMEM((R * C, 4, own, LANES), f32),
        pltpu.VMEM((R, own, DC), f32),
        pltpu.VMEM((R, own, DC), f32),
        pltpu.VMEM((C, T, F), f32),
        pltpu.VMEM((C, 2, own, LANES), f32),
        pltpu.VMEM((T, F), bf16),
        pltpu.VMEM((own, DC), bf16),
        dma((N,)), dma((7,)),
        dma((R,)), dma((R,)),
        dma((R * C,)), dma((R * C,)),
        dma((N, R)), dma((N, R)),
        dma((C,)), dma((C,)),
        dma((C,)), dma((C,)),
        dma((3,)), dma((3,)),
    ]
    flops = 4 * T * F * DC
    moved = 2 * DC * F
    return pl.pallas_call(
        functools.partial(kernel, (S, R, C, own, T, F, DC, N)),
        out_shape=[
            jax.ShapeDtypeStruct(act_in.shape, bf16),
            jax.ShapeDtypeStruct(hid_in.shape, bf16),
            jax.ShapeDtypeStruct(grad_in.shape, bf16),
        ],
        in_specs=[pl.BlockSpec(memory_space=pltpu.HBM)] * 8,
        out_specs=[pl.BlockSpec(memory_space=pl.ANY)] * 3,
        scratch_shapes=scratch,
        compiler_params=pltpu.CompilerParams(
            collective_id=0, has_side_effects=True, vmem_limit_bytes=40 * 2**20
        ),
        cost_estimate=pl.CostEstimate(flops=flops, bytes_accessed=moved, transcendentals=T * F),
    )(*arguments)


def solution(mesh):
    S, R, C = (mesh.shape[name] for name in ("section", "row", "col"))
    in_specs = (
        P("section", "row", "col"),
        P("section", None, "row"),
        P("section", "row", "col"),
        P("section", "row", "col"),
        P("section", None, "row"),
        P("section", "col", "row"),
        P(None, "col"),
        P(None, "col"),
    )
    out_specs = (P("section", "row", "col"), P("section", None, "row"), P("section", "row", "col"))
    return jax.shard_map(
        functools.partial(per_device, S, R, C),
        mesh=mesh, in_specs=in_specs, out_specs=out_specs, check_vma=False,
    )
```

time: 79.4 us -> 26.6 us (0.34)
  waiting for transfers between devices: 31.9 us -> 0 us
  Pallas kernels: 0 us -> 16.1 us
  blocking collectives: 15.6 us -> 0 us
  between operations: 14.9 us -> 0.66 us
  matrix products: 7.45 us -> 0 us
  local copies, waits for them, and re-layouts: 2.53 us -> 9.33 us
  starting transfers between devices: 3.99 us -> 0 us
  other arithmetic: 2.8 us -> 0 us
    unnamed x2 -> x0, waiting for transfers between devices: 28.3 us -> none
    pallas_call x0 -> x1, Pallas kernels: none -> 16.1 us  [per_device(): pl.pallas_call(functools.partial(kernel, (S, R, C, own, T, F, DC, N)), ou...]
    all_gather x1 -> x0, blocking collectives: 9.7 us -> none  [per_device(): lax.all_gather(leading, 'row', axis=0, tiled=True)]
    dot_general x2 -> x0, matrix products: 7.45 us -> none  [the longest x1 4.4 us: per_device(): lax.dot_general(right_side, weight, (((1,), (1,)), ((), ())), preferred_e...]
    unnamed x17 -> x19, local copies, waits for them, and re-layouts: 2.48 us -> 9.33 us
    psum x2 -> x0, blocking collectives: 5.88 us -> none  [col_total(): return lax.psum(values, 'col')]
    ppermute x3 -> x0, starting transfers between devices: 3.95 us -> none  [the longest x2 3.88 us: passed_along(): return lax.ppermute(block, axis, route)]
    ppermute x3 -> x0, waiting for transfers between devices: 3.62 us -> none  [the longest x1 3.62 us: partner(): lax.ppermute(shard, axis, [(i, i ^ 1 << stride) for i in range(lax.axis_s...]
  transfers between devices with their start and end apart: 4 -> 0, of which waited for: 2 -> 0; matrix products, arithmetic and copies ran while one was open for 5% -> 0% of each run, Pallas kernels for 0% -> 0%
where the time goes in v1:
time: 26.6 us; the launch traced here: 26.1 us
  Pallas kernels  16.1 us (61%)
  local copies, waits for them, and re-layouts  9.33 us (35%)
  between operations  0.66 us (2%)
    pallas_call x1, Pallas kernels, per_device(): pl.pallas_call(functools.partial(kernel, (S, R, C, own, T, F, DC, N)), ou...  16.1 us
    unnamed x19, local copies, waits for them, and re-layouts  9.33 us

profile of v1, /device:TPU:0, one launch (start us, length us, event | category | flops | bytes accessed | tf_op | source)
XLA Modules:
  0.0 26.1 jit_solution(16057306185549538270)
XLA Ops:
  0.6 0.0 copy-start
  0.6 2.3 %copy-done = bf16[1,6144,384]{2,1,0:T(8,128)(2,1)S(1)} copy-done((bf16[1,6144,384]{2,1,0:T(8,128)(2,1)S(1)}, bf16[1,6144,384]{2,1,0:T(8,128)(2,1)}, u32[]{:S(2)}) %copy-start) | copy-done | bytes 4718616
  3.0 0.0 copy-start.1
  3.0 0.8 %copy-done.1 = f32[2,6144]{1,0:T(2,128)S(1)} copy-done((f32[2,6144]{1,0:T(2,128)S(1)}, f32[2,6144]{1,0:T(2,128)}, u32[]{:S(2)}) %copy-start.1) | copy-done | bytes 49176
  3.8 0.0 copy-start.2
  3.8 0.8 %copy-done.2 = f32[2,6144]{1,0:T(2,128)S(1)} copy-done((f32[2,6144]{1,0:T(2,128)S(1)}, f32[2,6144]{1,0:T(2,128)}, u32[]{:S(2)}) %copy-start.2) | copy-done | bytes 49176
  4.6 0.0 copy-start.3
  4.6 0.7 %copy-done.3 = bf16[1,2,6144]{2,1,0:T(2,128)(2,1)S(1)} copy-done((bf16[1,2,6144]{2,1,0:T(2,128)(2,1)S(1)}, bf16[1,2,6144]{2,1,0:T(2,128)(2,1)}, u32[]{:S(2)}) %copy-start.3) | copy-done | bytes 24600
  5.3 0.0 copy-start.4
  5.3 0.7 %copy-done.4 = bf16[1,2,6144]{2,1,0:T(2,128)(2,1)S(1)} copy-done((bf16[1,2,6144]{2,1,0:T(2,128)(2,1)S(1)}, bf16[1,2,6144]{2,1,0:T(2,128)(2,1)}, u32[]{:S(2)}) %copy-start.4) | copy-done | bytes 24600
  6.0 0.0 copy-start.5
  6.0 0.7 %copy-done.5 = bf16[1,2,6144]{2,1,0:T(2,128)(2,1)S(1)} copy-done((bf16[1,2,6144]{2,1,0:T(2,128)(2,1)S(1)}, bf16[1,2,6144]{2,1,0:T(2,128)(2,1)}, u32[]{:S(2)}) %copy-start.5) | copy-done | bytes 24600
  6.8 0.0 copy-start.6
  6.8 0.7 %copy-done.6 = bf16[1,8,384]{2,1,0:T(8,128)(2,1)S(1)} copy-done((bf16[1,8,384]{2,1,0:T(8,128)(2,1)S(1)}, bf16[1,8,384]{2,1,0:T(8,128)(2,1)}, u32[]{:S(2)}) %copy-start.6) | copy-done | bytes 6168
  7.5 0.0 copy-start.7
  7.5 0.7 %copy-done.7 = bf16[1,8,384]{2,1,0:T(8,128)(2,1)S(1)} copy-done((bf16[1,8,384]{2,1,0:T(8,128)(2,1)S(1)}, bf16[1,8,384]{2,1,0:T(8,128)(2,1)}, u32[]{:S(2)}) %copy-start.7) | copy-done | bytes 6168
  8.2 16.1 %shard_map.103 = (bf16[1,2,6144]{2,1,0:T(2,128)(2,1)S(1)}, bf16[1,8,384]{2,1,0:T(8,128)(2,1)S(1)}, bf16[1,2,6144]{2,1,0:T(2,128)(2,1)S(1)}) custom-call(bf16[1,2,6144]{2,1,0:T(2,128)(2,1)S(1)} %copy-done.3, bf16[1,8,384]{2,1,0:T(8,128)(2,1)S(1)} %copy-done.6, bf16[1,2,6144]{2,1,0:T(2,128)(2,1)S(1)} %copy-done.4, bf16[1,2,6144]{2,1,0:T(2,128)(2,1)S(1)} %copy-done.5, ...), custom_call_target="tpu_custom_call" | custom-call | flops 75497472 | bytes 4718592 | tf_op jit(solution)/shard_map/pallas_call | solution.py:343
  24.3 0.6 %copy.14 = bf16[1,2,6144]{2,1,0:T(2,128)(2,1)} copy(bf16[1,2,6144]{2,1,0:T(2,128)(2,1)S(1)} %get-tuple-element.6) | data formatting | bytes 49152
  24.9 0.6 %copy.15 = bf16[1,8,384]{2,1,0:T(8,128)(2,1)} copy(bf16[1,8,384]{2,1,0:T(8,128)(2,1)S(1)} %get-tuple-element.7) | data formatting | bytes 12288
  25.5 0.6 %copy.16 = bf16[1,2,6144]{2,1,0:T(2,128)(2,1)} copy(bf16[1,2,6144]{2,1,0:T(2,128)(2,1)S(1)} %get-tuple-element.8) | data formatting | bytes 49152
Async XLA Ops:
  0.6 2.3 %copy-start = (bf16[1,6144,384]{2,1,0:T(8,128)(2,1)S(1)}, bf16[1,6144,384]{2,1,0:T(8,128)(2,1)}, u32[]{:S(2)}) copy-start(bf16[1,6144,384]{2,1,0:T(8,128)(2,1)} %weights.1) | copy-start | bytes 14155780
  3.0 0.8 %copy-start.1 = (f32[2,6144]{1,0:T(2,128)S(1)}, f32[2,6144]{1,0:T(2,128)}, u32[]{:S(2)}) copy-start(f32[2,6144]{1,0:T(2,128)} %gain_in.1) | copy-start | bytes 147460
  3.8 0.8 %copy-start.2 = (f32[2,6144]{1,0:T(2,128)S(1)}, f32[2,6144]{1,0:T(2,128)}, u32[]{:S(2)}) copy-start(f32[2,6144]{1,0:T(2,128)} %bias_in.1) | copy-start | bytes 147460
  4.6 0.7 %copy-start.3 = (bf16[1,2,6144]{2,1,0:T(2,128)(2,1)S(1)}, bf16[1,2,6144]{2,1,0:T(2,128)(2,1)}, u32[]{:S(2)}) copy-start(bf16[1,2,6144]{2,1,0:T(2,128)(2,1)} %act_in.1) | copy-start | bytes 73732
  5.3 0.7 %copy-start.4 = (bf16[1,2,6144]{2,1,0:T(2,128)(2,1)S(1)}, bf16[1,2,6144]{2,1,0:T(2,128)(2,1)}, u32[]{:S(2)}) copy-start(bf16[1,2,6144]{2,1,0:T(2,128)(2,1)} %grad_in.1) | copy-start | bytes 73732
  6.0 0.7 %copy-start.5 = (bf16[1,2,6144]{2,1,0:T(2,128)(2,1)S(1)}, bf16[1,2,6144]{2,1,0:T(2,128)(2,1)}, u32[]{:S(2)}) copy-start(bf16[1,2,6144]{2,1,0:T(2,128)(2,1)} %saved_in.1) | copy-start | bytes 73732
  6.8 0.7 %copy-start.6 = (bf16[1,8,384]{2,1,0:T(8,128)(2,1)S(1)}, bf16[1,8,384]{2,1,0:T(8,128)(2,1)}, u32[]{:S(2)}) copy-start(bf16[1,8,384]{2,1,0:T(8,128)(2,1)} %hid_in.1) | copy-start | bytes 18436
  7.5 0.7 %copy-start.7 = (bf16[1,8,384]{2,1,0:T(8,128)(2,1)S(1)}, bf16[1,8,384]{2,1,0:T(8,128)(2,1)}, u32[]{:S(2)}) copy-start(bf16[1,8,384]{2,1,0:T(8,128)(2,1)} %pre_in.1) | copy-start | bytes 18436

commit v2 on v1

--- a/solution.py
+++ b/solution.py
@@ -12,6 +12,7 @@
 CUBIC = 0.044715
 MESH = pl.DeviceIdType.MESH
 LANES = 128
+LIMIT = 64 * 2**20
 
 
 def each(count, body):
@@ -301,6 +302,15 @@
     def _():
         each(R * C - 1, lambda k: stat_copy(k).wait_send())
         each(C - 1, lambda k: mom_copy(k).wait_send())
+
+
+def write_out(a, b, c, a_out, b_out, c_out, sem):
+    pairs = ((a, a_out), (b, b_out), (c, c_out))
+    copies = [pltpu.make_async_copy(i, o, sem.at[k]) for k, (i, o) in enumerate(pairs)]
+    for copy in copies:
+        copy.start()
+    for copy in copies:
+        copy.wait()
 
 
 def per_device(S, R, C, *arguments):
@@ -340,7 +350,7 @@
     ]
     flops = 4 * T * F * DC
     moved = 2 * DC * F
-    return pl.pallas_call(
+    results = pl.pallas_call(
         functools.partial(kernel, (S, R, C, own, T, F, DC, N)),
         out_shape=[
             jax.ShapeDtypeStruct(act_in.shape, bf16),
@@ -351,10 +361,18 @@
         out_specs=[pl.BlockSpec(memory_space=pl.ANY)] * 3,
         scratch_shapes=scratch,
         compiler_params=pltpu.CompilerParams(
-            collective_id=0, has_side_effects=True, vmem_limit_bytes=40 * 2**20
+            collective_id=0, has_side_effects=True, vmem_limit_bytes=LIMIT
         ),
         cost_estimate=pl.CostEstimate(flops=flops, bytes_accessed=moved, transcendentals=T * F),
     )(*arguments)
+    return pl.pallas_call(
+        write_out,
+        out_shape=[jax.ShapeDtypeStruct(a.shape, a.dtype) for a in results],
+        in_specs=[pl.BlockSpec(memory_space=pl.ANY)] * 3,
+        out_specs=[pl.BlockSpec(memory_space=pl.ANY)] * 3,
+        scratch_shapes=[dma((3,))],
+        compiler_params=pltpu.CompilerParams(vmem_limit_bytes=LIMIT),
+    )(*results)
 
 
 def solution(mesh):

time: 26.6 us -> 19.6 us (0.74); the launches traced: 26.1 us -> 19.5 us
  local copies, waits for them, and re-layouts: 9.33 us -> 0 us
  Pallas kernels: 16.1 us -> 18.8 us
    unnamed x19 -> x0, local copies, waits for them, and re-layouts: 9.33 us -> none
    pallas_call x0 -> x1, Pallas kernels: none -> 2.81 us  [per_device(): pl.pallas_call(write_out, out_shape=[jax.ShapeDtypeStruct(a.shape, a.dtyp...]
where the time goes in v2:
time: 19.6 us; the launch traced here: 19.5 us
  Pallas kernels  18.8 us (96%)
  between operations  0.64 us (3%)
    pallas_call x1, Pallas kernels, per_device(): pl.pallas_call(functools.partial(kernel, (S, R, C, own, T, F, DC, N)), ou...  16 us
    pallas_call x1, Pallas kernels, per_device(): pl.pallas_call(write_out, out_shape=[jax.ShapeDtypeStruct(a.shape, a.dtyp...  2.81 us

profile of v2, /device:TPU:0, one launch (start us, length us, event | category | flops | bytes accessed | tf_op | source)
XLA Modules:
  0.0 19.5 jit_solution(3848125700591587965)
XLA Ops:
  0.6 16.0 %shard_map.103 = (bf16[1,2,6144]{2,1,0:T(2,128)(2,1)}, bf16[1,8,384]{2,1,0:T(8,128)(2,1)}, bf16[1,2,6144]{2,1,0:T(2,128)(2,1)}) custom-call(bf16[1,2,6144]{2,1,0:T(2,128)(2,1)} %act_in.1, bf16[1,8,384]{2,1,0:T(8,128)(2,1)} %hid_in.1, bf16[1,2,6144]{2,1,0:T(2,128)(2,1)} %grad_in.1, bf16[1,2,6144]{2,1,0:T(2,128)(2,1)} %saved_in.1, bf16[1,8,384]{2,1,0:T(8,128)(2,1)} %pre_in.1, ...), custom_call_target="tpu_custom_call" | custom-call | flops 75497472 | bytes 4718592 | tf_op jit(solution)/shard_map/pallas_call | solution.py:353
  16.7 2.8 %shard_map.104 = (bf16[1,2,6144]{2,1,0:T(2,128)(2,1)}, bf16[1,8,384]{2,1,0:T(8,128)(2,1)}, bf16[1,2,6144]{2,1,0:T(2,128)(2,1)}) custom-call(bf16[1,2,6144]{2,1,0:T(2,128)(2,1)} %get-tuple-element.6.a, bf16[1,8,384]{2,1,0:T(8,128)(2,1)} %get-tuple-element.7.b, bf16[1,2,6144]{2,1,0:T(2,128)(2,1)} %get-tuple-element.8.c), custom_call_target="tpu_custom_call" | custom-call | tf_op jit(solution)/shard_map/pallas_call | solution.py:368

commit v3 on v2

--- a/solution.py
+++ b/solution.py
@@ -12,7 +12,7 @@
 CUBIC = 0.044715
 MESH = pl.DeviceIdType.MESH
 LANES = 128
-LIMIT = 64 * 2**20
+LIMIT = 48 * 2**20
 
 
 def each(count, body):
@@ -353,18 +353,18 @@
     results = pl.pallas_call(
         functools.partial(kernel, (S, R, C, own, T, F, DC, N)),
         out_shape=[
-            jax.ShapeDtypeStruct(act_in.shape, bf16),
-            jax.ShapeDtypeStruct(hid_in.shape, bf16),
-            jax.ShapeDtypeStruct(grad_in.shape, bf16),
+            pltpu.VMEM(act_in.shape, bf16),
+            pltpu.VMEM(hid_in.shape, bf16),
+            pltpu.VMEM(grad_in.shape, bf16),
         ],
-        in_specs=[pl.BlockSpec(memory_space=pltpu.HBM)] * 8,
+        in_specs=[pl.BlockSpec(memory_space=pl.ANY)] * 8,
         out_specs=[pl.BlockSpec(memory_space=pl.ANY)] * 3,
         scratch_shapes=scratch,
         compiler_params=pltpu.CompilerParams(
             collective_id=0, has_side_effects=True, vmem_limit_bytes=LIMIT
         ),
         cost_estimate=pl.CostEstimate(flops=flops, bytes_accessed=moved, transcendentals=T * F),
-    )(*arguments)
+    )(*(pltpu.with_memory_space_constraint(a, pltpu.HBM) for a in arguments))
     return pl.pallas_call(
         write_out,
         out_shape=[jax.ShapeDtypeStruct(a.shape, a.dtype) for a in results],

time: 19.6 us -> 17.4 us (0.89)
  Pallas kernels: 18.8 us -> 16.6 us
    pallas_call x1, Pallas kernels: 2.81 us -> 0.65 us  [per_device(): pl.pallas_call(write_out, out_shape=[jax.ShapeDtypeStruct(a.shape, a.dtyp...]
where the time goes in v3:
time: 17.4 us; the launch traced here: 17.2 us
  Pallas kernels  16.6 us (95%)
  between operations  0.64 us (4%)
    pallas_call x1, Pallas kernels, per_device(): pl.pallas_call(functools.partial(kernel, (S, R, C, own, T, F, DC, N)), ou...  15.9 us
    pallas_call x1, Pallas kernels, per_device(): pl.pallas_call(write_out, out_shape=[jax.ShapeDtypeStruct(a.shape, a.dtyp...  0.65 us

profile of v3, /device:TPU:0, one launch (start us, length us, event | category | flops | bytes accessed | tf_op | source)
XLA Modules:
  0.0 17.2 jit_solution(6186549027142031901)
XLA Ops:
  0.6 15.9 %shard_map.103 = (bf16[1,2,6144]{2,1,0:T(2,128)(2,1)S(1)}, bf16[1,8,384]{2,1,0:T(8,128)(2,1)S(1)}, bf16[1,2,6144]{2,1,0:T(2,128)(2,1)S(1)}) custom-call(bf16[1,2,6144]{2,1,0:T(2,128)(2,1)} %act_in.1, bf16[1,8,384]{2,1,0:T(8,128)(2,1)} %hid_in.1, bf16[1,2,6144]{2,1,0:T(2,128)(2,1)} %grad_in.1, bf16[1,2,6144]{2,1,0:T(2,128)(2,1)} %saved_in.1, ...), custom_call_target="tpu_custom_call" | custom-call | flops 75497472 | bytes 4718592 | tf_op jit(solution)/shard_map/pallas_call | solution.py:353
  16.6 0.6 %shard_map.104 = (bf16[1,2,6144]{2,1,0:T(2,128)(2,1)}, bf16[1,8,384]{2,1,0:T(8,128)(2,1)}, bf16[1,2,6144]{2,1,0:T(2,128)(2,1)}) custom-call(bf16[1,2,6144]{2,1,0:T(2,128)(2,1)S(1)} %get-tuple-element.6.a, bf16[1,8,384]{2,1,0:T(8,128)(2,1)S(1)} %get-tuple-element.7.b, bf16[1,2,6144]{2,1,0:T(2,128)(2,1)S(1)} %get-tuple-element.8.c), custom_call_target="tpu_custom_call" | custom-call | tf_op jit(solution)/shard_map/pallas_call | solution.py:368
